TPU v7x, 512 devices: a whole 4x8x8 slice. The times are simulated.
512 devices in a mesh: kv: 64 (over y, z), tp: 8 (over x, core).
Axes of the slice: x: 4, y: 8, z: 8, core: 2. Of those that a mesh axis runs over, the one named last changes fastest.
Arguments:
- queries: bfloat16 [1024, 2048], P('kv', 'tp'), may hold values from -6 to 6
- prefix_ids: int32 [1024, 1], P('kv'), may hold values from 0 to 7, as said below
- prefix_kv: bfloat16 [2, 131072, 1024], P(None, 'kv', 'tp'), may hold values from -6 to 6
- prefix_scales: float32 [2, 8, 131072], P(None, 'tp', 'kv'), may hold values from 0.5 to 2
- suffix_kv: bfloat16 [2, 1024, 128, 1024], P(None, 'kv', None, 'tp'), may hold values from -9 to 9
- suffix_lengths: int32 [1024], P('kv'), may hold values from 1 to 128
- out_weight: bfloat16 [2048, 4608], P('tp'), may hold values from -1.41421356 to 1.41421356
- residual: bfloat16 [1024, 4608], P('kv', 'tp'), may hold values from -6 to 6
- norm_gain: float32 [4608], P('tp'), may hold values from 0.1 to 1.9
Outputs:
- mixed: bfloat16 [1024, 4608], P('kv', 'tp')
Inputs may be any that keep to these rules, and one draw needn't show every extreme that they name: `prefix_ids`: among the 16 requests of one index of kv at most 6 have any one prefix; in every draw one prefix has exactly 6 requests on every index of kv.
All inputs are finite; a program needn't handle non-finite values.
Results may differ from a plain program's by a relative error of at most 0.0049.
Values may be sent and summed in bfloat16 or wider, within the bound.
A program may use at most 64 MiB of HBM per device.

v0:
```python
import math

import jax
import jax.numpy as jnp
from jax import lax
from jax.sharding import PartitionSpec as P

HD = 128
NPRE = 8


score_scale = 144.0 ** (-0.5)


def capped(raw_scores):
    return 50.0 * jnp.tanh(raw_scores / 50.0)


def prefix_terms(query_rows, prefix_kv, prefix_scales, head_size):
    local_heads = prefix_scales.shape[1]
    group_size = query_rows.shape[1] // (local_heads * head_size)
    row_count = query_rows.shape[0]
    head_rows = query_rows
    head_rows = head_rows.reshape(row_count * group_size, head_size)
    columns = slice(0, head_size)
    raw_scores = lax.dot_general(
        head_rows,
        prefix_kv[0, :, columns],
        (((1,), (1,)), ((), ())),
        preferred_element_type=jnp.float32,
    )
    scores = capped(raw_scores * prefix_scales[0, 0][None, :] * score_scale)
    exponent = jnp.exp(scores)
    row_total = jnp.sum(exponent, axis=1)
    weights = (exponent * prefix_scales[1, 0][None, :]).astype(jnp.bfloat16)
    head_out = jnp.dot(weights, prefix_kv[1, :, columns], preferred_element_type=jnp.float32)
    pieces = [head_out.reshape(row_count, group_size * head_size)]
    totals = [row_total.reshape(row_count, group_size)]
    return (jnp.concatenate(pieces, axis=1), jnp.concatenate(totals, axis=1))


def suffix_terms(queries, suffix_kv, suffix_lengths, head_size):
    row_count = queries.shape[0]
    span = suffix_kv.shape[2]
    local_heads = suffix_kv.shape[3] // head_size
    group_size = queries.shape[1] // (local_heads * head_size)
    query_four = queries.reshape(row_count, local_heads, group_size, head_size)
    key_four = suffix_kv[0].reshape(row_count, span, local_heads, head_size)
    value_four = suffix_kv[1].reshape(row_count, span, local_heads, head_size)
    raw_scores = jnp.einsum(
        "rgid,rsgd->rgis", query_four, key_four, preferred_element_type=jnp.float32
    )
    scores = capped(raw_scores * score_scale)
    position = lax.broadcasted_iota(jnp.int32, (1, 1, 1, span), 3)
    live = position < suffix_lengths[:, None, None, None]
    exponent = jnp.where(live, jnp.exp(scores), jnp.float32(0.0))
    totals = jnp.sum(exponent, axis=3).reshape(row_count, local_heads * group_size)
    head_out = jnp.einsum(
        "rgis,rsgd->rgid",
        exponent.astype(jnp.bfloat16),
        value_four,
        preferred_element_type=jnp.float32,
    )
    return (head_out.reshape(row_count, local_heads * group_size * head_size), totals)


def local(
    queries,
    prefix_ids,
    prefix_kv,
    prefix_scales,
    suffix_kv,
    suffix_lengths,
    out_weight,
    residual,
    norm_gain,
):
    row_count = queries.shape[0]
    feature_count = queries.shape[1]
    local_heads = out_weight.shape[0] // HD
    owners = lax.axis_size("kv") // NPRE
    suffix_out, suffix_total = suffix_terms(queries, suffix_kv, suffix_lengths, HD)
    request_prefix = prefix_ids[:, 0]
    gathered, gathered_ids = (
        lax.all_gather(queries, "kv", axis=0, tiled=True),
        lax.all_gather(request_prefix.astype(jnp.bfloat16), "kv", axis=0, tiled=True),
    )
    all_rows = gathered.shape[0]
    block_rows = math.gcd(all_rows, 256)
    block_count = all_rows // block_rows

    def block_terms(block):
        return prefix_terms(block, prefix_kv, prefix_scales, HD)

    block_out, block_total = lax.map(
        block_terms, gathered.reshape(block_count, block_rows, feature_count)
    )
    own_prefix = (lax.axis_index("kv") // owners).astype(jnp.bfloat16)
    keep = (gathered_ids == own_prefix)[:, None]
    all_out = jnp.where(keep, block_out.reshape(all_rows, feature_count), jnp.float32(0.0))
    all_total = jnp.where(keep, block_total.reshape(all_rows, local_heads), jnp.float32(0.0))
    prefix_out, prefix_total = (
        lax.psum_scatter(all_out, "kv", scatter_dimension=0, tiled=True),
        lax.psum_scatter(all_total, "kv", scatter_dimension=0, tiled=True),
    )
    combined = (prefix_out + suffix_out).reshape(row_count, local_heads, HD)
    denominator = (prefix_total + suffix_total)[:, :, None]
    attention = (combined / denominator).reshape(row_count, feature_count).astype(jnp.bfloat16)
    partial_projection = jnp.dot(attention, out_weight, preferred_element_type=jnp.float32)
    own_width = norm_gain.shape[0]
    own_projection = lax.psum_scatter(partial_projection, "tp", scatter_dimension=1, tiled=True)
    square_sum = lax.psum(jnp.sum(own_projection * own_projection, axis=1), "tp")
    mean_square = square_sum / (own_width * lax.axis_size("tp"))
    normed = own_projection * lax.rsqrt(mean_square + 1e-06)[:, None] * norm_gain[None, :]
    return (residual.astype(jnp.float32) + normed).astype(jnp.bfloat16)


def solution(mesh):
    placed = (
        P("kv", "tp"),
        P("kv", None),
        P(None, "kv", "tp"),
        P(None, "tp", "kv"),
        P(None, "kv", None, "tp"),
        P("kv"),
        P("tp", None),
        P("kv", "tp"),
        P("tp"),
    )
    return jax.shard_map(
        local, mesh=mesh, in_specs=placed, out_specs=P("kv", "tp"), check_vma=False
    )
```

profile of v0, /device:TPU:448, one launch (start us, length us, event | category | flops | bytes accessed | tf_op | source)
XLA Modules:
  0.0 526.4 jit_solution(4780153626578378831)
XLA Ops:
  6.5 49.7 %all_gather.7 = bf16[1024,256]{1,0:T(8,128)(2,1)S(1)} all-gather(bf16[16,256]{1,0:T(8,128)(2,1)} %param.11), channel_id=1, replica_groups=mesh['kv'=64,'tp'=8] {'kv'}, dimensions={0}, use_global_device_ids=true | all-gather | bytes 532480 | tf_op jit(solution)/shard_map/all_gather | solution.py:85
  56.2 22.9 %while.14 = (s32[]{:T(128)}, f32[4,256,256]{2,1,0:T(8,128)}, f32[4,256,2]{2,1,0:T(8,128)}, bf16[4,256,256]{2,1,0:T(8,128)(2,1)S(1)}, bf16[2,2048,128]{2,1,0:T(8,128)(2,1)}, /*index=5*/f32[2,1,2048]{2,1,0:T(1,128)}, s32[]{:T(128)}) while((s32[]{:T(128)}, f32[4,256,256]{2,1,0:T(8,128)}, f32[4,256,2]{2,1,0:T(8,128)}, ...), condition=%wide.region_2.3_spmd, body=%wide.region_0.0_spmd.sunk | while | flops 543161856 | bytes 15786109 | solution.py:95
  56.2 0.7 fusion.33
  57.1 2.6 fusion.34
  59.6 0.7 fusion.35
  60.4 0.7 constant_dynamic-update-slice_fusion.4
  61.3 0.7 constant_dynamic-update-slice_fusion.5
  62.0 0.7 fusion.33
  62.8 2.6 fusion.34
  65.4 0.7 fusion.35
  66.2 0.7 constant_dynamic-update-slice_fusion.4
  67.7 0.7 fusion.33
  68.5 2.6 fusion.34
  71.1 0.7 fusion.35
  71.9 0.7 constant_dynamic-update-slice_fusion.4
  73.4 0.7 fusion.33
  74.2 2.6 fusion.34
  76.8 0.7 fusion.35
  77.6 0.7 constant_dynamic-update-slice_fusion.4
  78.5 0.7 constant_dynamic-update-slice_fusion.5
  79.2 0.7 fusion.20
  80.8 129.6 %all-reduce = bf16[1024]{0:T(1024)(128)(2,1)S(1)} all-reduce(bf16[1024]{0:T(1024)(128)(2,1)S(1)} %dynamic-update-slice), channel_id=2, replica_groups=mesh['kv'=64,'tp'=8] {'kv'}, use_global_device_ids=true, to_apply=%add | all-reduce | flops 1024 | bytes 4096
  210.4 2.5 bitcast_select_fusion
  213.0 1.2 copy.14
  214.9 142.8 %all-reduce.1 = f32[1024,2]{0,1:T(2,128)S(1)} all-reduce(f32[1024,2]{0,1:T(2,128)S(1)} %broadcast_select_fusion), channel_id=4, replica_groups=mesh['kv'=64,'tp'=8] {'kv'}, use_global_device_ids=true, to_apply=%region_4.5.clone | all-reduce | flops 2048 | bytes 16384
  357.9 1.5 fusion.21
  359.7 102.9 %reduce-scatter.6.cloned.1.call-done = f32[16,256]{1,0:T(8,128)} async-done(((f32[1024,256]{1,0:T(8,128)}), f32[16,256]{1,0:T(8,128)}) %reduce-scatter.6.cloned.1.call-update) | async-done | bytes 16400 | tf_op jit(solution)/shard_map/reduce_scatter | solution.py:103
  462.7 3.2 convolution_bitcast_fusion
  465.9 38.9 %reduce-scatter.8.cloned.1.call-done = f32[576,16]{1,0:T(8,128)} async-done(((f32[4608,16]{1,0:T(8,128)}), f32[576,16]{1,0:T(8,128)}) %reduce-scatter.8.cloned.1.call-update) | async-done | bytes 36880
  504.7 1.1 copy.18
  506.0 12.9 %psum.7 = f32[16]{0:T(128)S(1)} all-reduce(f32[16]{0:T(128)S(1)} %multiply_reduce_fusion), channel_id=1, replica_groups=mesh['kv'=64,'tp'=8] {'tp'}, use_global_device_ids=true, to_apply=%region_8.9 | all-reduce | flops 16 | bytes 128 | tf_op jit(solution)/shard_map/psum | solution.py:112
  518.9 0.7 add_convert_fusion
  (62 shorter events, 3.5 us)
Async XLA Ops:
  6.5 456.1 %copy-start = (bf16[256,4608]{1,0:T(8,128)(2,1)S(1)}, bf16[256,4608]{1,0:T(8,128)(2,1)}, u32[]{:S(2)}) copy-start(bf16[256,4608]{1,0:T(8,128)(2,1)} %param.17) | copy-start | bytes 7077892
  6.5 456.0 %reduce-scatter.6.cloned.1.call-start = ((), (), s32[]{:S(2)}) async-start(), calls=%async_computation.2 | async-start | bytes 1064960 | tf_op jit(solution)/shard_map/reduce_scatter | solution.py:103
  56.2 23.0 %copy-start.8 = (s32[16,1]{0,1:T(1,128)S(1)}, s32[16,1]{0,1:T(1,128)}, u32[]{:S(2)}) copy-start(s32[16,1]{0,1:T(1,128)} %param.12) | copy-start | bytes 196
  56.2 23.0 %copy-start.6 = (u32[512]{0:T(512)S(1)}, u32[512]{0:T(512)}, u32[]{:S(2)}) copy-start(u32[512]{0:T(512)} %constant.84) | copy-start | bytes 6148
  56.2 156.8 %copy-start.3 = (bf16[16,256]{1,0:T(8,128)(2,1)S(1)}, bf16[16,256]{1,0:T(8,128)(2,1)}, u32[]{:S(2)}) copy-start(bf16[16,256]{1,0:T(8,128)(2,1)} %param.11) | copy-start | bytes 24580
  56.2 301.6 %copy-start.7 = (s32[16]{0:T(128)S(1)}, s32[16]{0:T(128)}, u32[]{:S(2)}) copy-start(s32[16]{0:T(128)} %param.16) | copy-start | bytes 196
  57.0 2.6 copy-start.1
  62.8 2.6 copy-start.1
  68.5 2.6 copy-start.1
  74.2 2.6 copy-start.1
  79.2 280.3 %copy-start.2 = (bf16[2,16,128,128]{3,2,1,0:T(8,128)(2,1)S(1)}, bf16[2,16,128,128]{3,2,1,0:T(8,128)(2,1)}, u32[]{:S(2)}) copy-start(bf16[2,16,128,128]{3,2,1,0:T(8,128)(2,1)} %param.15) | copy-start | bytes 3145732
  212.9 291.8 %reduce-scatter.8.cloned.1.call-start = ((), (), s32[]{:S(2)}) async-start(), calls=%async_computation.3 | async-start | bytes 2654208
  359.4 159.4 %copy-start.4 = (bf16[16,576]{1,0:T(8,128)(2,1)S(1)}, bf16[16,576]{1,0:T(8,128)(2,1)}, u32[]{:S(2)}) copy-start(bf16[16,576]{1,0:T(8,128)(2,1)} %param.18) | copy-start | bytes 55300
  359.4 159.4 %copy-start.5 = (f32[576]{0:T(1024)S(1)}, f32[576]{0:T(1024)}, u32[]{:S(2)}) copy-start(f32[576]{0:T(1024)} %param.19) | copy-start | bytes 6916
Sparse Core Ops, SparseCore 0:
  213.0 249.5 reduce-scatter.5
  466.0 38.6 reduce-scatter.7
where the time goes:
time: 533 us; the launch traced here: 526 us
  blocking collectives  335 us (63%)
  waiting for transfers between devices  142 us (27%)
  matrix products  18.2 us (3%)
  between operations  14.9 us (3%)
  local copies, waits for them, and re-layouts  13 us (2%)
    unnamed x2, blocking collectives  272 us
    reduce_scatter x1, waiting for transfers between devices, local(): lax.psum_scatter(all_out, 'kv', scatter_dimension=0, tiled=True)  103 us
    all_gather x1, blocking collectives, local(): lax.all_gather(queries, 'kv', axis=0, tiled=True)  49.7 us
    unnamed x3, waiting for transfers between devices  38.9 us
    psum x1, blocking collectives, local(): lax.psum(jnp.sum(own_projection * own_projection, axis=1), 'tp')  12.9 us
  transfers between devices with their start and end apart: 2, of which 2 were waited for; matrix products, arithmetic and copies ran while one was open for 1% of the time, Pallas kernels for 0%

commit v1 on v0

v1 whole, which is shorter than its diff:
```python
import jax
import jax.numpy as jnp
from jax import lax
from jax.experimental import pallas as pl
from jax.experimental.pallas import tpu as pltpu
from jax.sharding import PartitionSpec as P

HD = 128
NPRE = 8
SLOTS = 6
SLAB = 16
MESH = pl.DeviceIdType.MESH
BF = jnp.bfloat16
F32 = jnp.float32
LOG2E = 1.4426950408889634
SCORE = 144.0 ** (-0.5)
CHUNK = 256


def iota(shape, dim):
    return lax.broadcasted_iota(jnp.int32, shape, dim)


def nt(a, b):
    return lax.dot_general(a, b, (((1,), (1,)), ((), ())), preferred_element_type=F32)


def mm(a, b):
    return jnp.dot(a, b, preferred_element_type=F32)


def split(a):
    high = a.astype(BF)
    return high, (a - high.astype(F32)).astype(BF)


def kernel(
    nz, ny, nx,
    q_ref, ids_ref, kv_ref, scales_ref, suf_ref, len_ref, w_ref, res_ref, gain_ref,
    o_ref,
    q_v, kv_v, sc_v, suf_v, w_v, res_v, gain_v,
    slots, gathered, blocks, msgs, back, part, parts, square, squares, out_v,
    local_sem, go_y, go_z, sy, ry, sz, rz, sr, rr, sx, rx, ss, rs,
):
    kv, tp = lax.axis_index("kv"), lax.axis_index("tp")
    y, z = lax.div(kv, nz), lax.rem(kv, nz)
    x, core = lax.div(tp, 2), lax.rem(tp, 2)

    barrier = pltpu.get_barrier_semaphore()

    def here(to_kv, to_tp):
        pl.semaphore_signal(barrier, inc=1, device_id=(to_kv, to_tp), device_id_type=MESH)

    here(kv, x * 2 + (1 - core))
    for i in (4, 3, 5, 2, 6, 1, 7):
        here(y * nz + lax.rem(z + i, nz), x * 2 + 1)
    for i in (4, 3, 5, 2, 6, 1, 7):
        here(lax.rem(y + i, ny) * nz + z, x * 2)
    for i in (2, 1, 3):
        here(kv, lax.rem(x + i, nx) * 2 + 1)

    def fetch(i, src, dst):
        c = pltpu.make_async_copy(src, dst, local_sem.at[i])
        c.start()
        return c

    got_q = fetch(0, q_ref, q_v)
    got_kv = fetch(1, kv_ref, kv_v)
    got_sc = fetch(2, scales_ref, sc_v)
    got_suf = fetch(3, suf_ref, suf_v)
    got_w = fetch(4, w_ref, w_v)
    got_res = fetch(5, res_ref, res_v)
    got_gain = fetch(6, gain_ref, gain_v)

    row16, lane16 = iota((16, 128), 0), iota((16, 128), 1)
    ids_row = ids_ref[...].astype(F32)
    square16 = iota((16, 16), 0), iota((16, 16), 1)
    ids = jnp.sum(jnp.where(square16[0] == square16[1], ids_row, 0.0), axis=1, keepdims=True)
    same = jnp.where(ids == ids_row, 1.0, 0.0)
    rank = jnp.sum(jnp.where(square16[1] < square16[0], same, 0.0), axis=1, keepdims=True)
    rank_row = jnp.sum(jnp.where(square16[0] < square16[1], same, 0.0), axis=0, keepdims=True)
    place = (ids * SLAB + rank).astype(jnp.int32)
    place_row = (ids_row * SLAB + rank_row).astype(jnp.int32)

    got_q.wait()
    row128 = iota((128, 16), 0)
    picks = [jnp.where(row128 == place_row + h * SLOTS, 1.0, 0.0).astype(BF) for h in range(2)]
    slotted = mm(picks[0], q_v[:, :HD]) + mm(picks[1], q_v[:, HD:])
    slots[...] = slotted.astype(BF).reshape(NPRE, SLAB, HD)

    @pl.when(core == 0)
    def _():
        pl.semaphore_wait(barrier, 2 * (ny - 1) + 1)
        pl.semaphore_signal(go_y, inc=1, device_id=(kv, tp + 1), device_id_type=MESH)

    @pl.when(core == 1)
    def _():
        pl.semaphore_wait(go_y, 1)

    def to_holder(i):
        p = lax.rem(y + i, ny)
        return pltpu.make_async_remote_copy(
            src_ref=slots.at[p], dst_ref=gathered.at[y], send_sem=sy.at[i], recv_sem=ry.at[y],
            device_id=(p * nz + z, tp), device_id_type=MESH,
        )

    for i in (4, 3, 5, 2, 6, 1, 7):
        to_holder(i).start()
    gathered[y] = slots[y]

    got_suf.wait()
    eye = jnp.where(iota((32, 16), 1) == lax.rem(iota((32, 16), 0), 16), 1.0, 0.0)
    lens = jnp.sum(eye * len_ref[...].astype(F32), axis=1, keepdims=True).astype(jnp.int32)
    own_q = jnp.concatenate([q_v[:, :HD], q_v[:, HD:]], axis=0)
    own_request = lax.rem(iota((32, CHUNK), 0), 16)
    suf_out = jnp.zeros((32, HD), F32)
    suf_total = jnp.zeros((32, 128), F32)
    for c in range(8):
        k = suf_v[0, 2 * c : 2 * c + 2].reshape(CHUNK, HD)
        v = suf_v[1, 2 * c : 2 * c + 2].reshape(CHUNK, HD)
        e = jnp.exp2(jnp.tanh(nt(own_q, k) * (SCORE / 50.0)) * (50.0 * LOG2E))
        at = iota((32, CHUNK), 1)
        live = (lax.div(at, 128) + 2 * c == own_request) & (lax.rem(at, 128) < lens)
        e = jnp.where(live, e, 0.0)
        suf_total += e[:, :128] + e[:, 128:]
        suf_out += mm(e.astype(BF), v)
    suf_total = jnp.sum(suf_total, axis=1, keepdims=True)

    got_kv.wait()
    got_sc.wait()
    sc_v[0] = sc_v[0] * (SCORE / 50.0)

    def from_source(i):
        return pltpu.make_async_remote_copy(
            src_ref=slots.at[i], dst_ref=gathered.at[i], send_sem=sy.at[i], recv_sem=ry.at[i],
            device_id=(kv, tp), device_id_type=MESH,
        )

    for i in range(1, ny):
        from_source(lax.rem(y + i, ny)).wait_recv()
    compact = jnp.where(
        iota((96, 128), 1) == lax.div(iota((96, 128), 0), 12) * SLAB + lax.rem(iota((96, 128), 0), 12), 1.0, 0.0
    ).astype(BF)
    blocks[z] = mm(compact, gathered[...].reshape(128, HD)).astype(BF)

    @pl.when(core == 1)
    def _():
        pl.semaphore_wait(barrier, 2 * (nz - 1) + 1 + 2 * (nx - 1))
        pl.semaphore_signal(go_z, inc=1, device_id=(kv, tp - 1), device_id_type=MESH)

    @pl.when(core == 0)
    def _():
        pl.semaphore_wait(go_z, 1)

    def along_row(i):
        return pltpu.make_async_remote_copy(
            src_ref=blocks.at[z], dst_ref=blocks.at[z], send_sem=sz.at[i], recv_sem=rz.at[z],
            device_id=(y * nz + lax.rem(z + i, nz), tp), device_id_type=MESH,
        )

    for i in (4, 3, 5, 2, 6, 1, 7):
        along_row(i).start()

    expand = jnp.where(
        (iota((128, 96), 1) == lax.div(iota((128, 96), 0), SLAB) * 12 + lax.rem(iota((128, 96), 0), SLAB))
        & (lax.rem(iota((128, 96), 0), SLAB) < 12),
        1.0, 0.0,
    ).astype(BF)
    ones = jnp.ones((128, 256), BF)
    in_slab = lax.rem(iota((128, 128), 0), SLAB)

    def back_to(b, i):
        to_y = lax.rem(y + i, ny)
        return pltpu.make_async_remote_copy(
            src_ref=msgs.at[b, to_y], dst_ref=back.at[z, y], send_sem=sr.at[b, i], recv_sem=rr.at[z, y],
            device_id=(to_y * nz + b, tp), device_id_type=MESH,
        )

    def one_block(b, carry):
        @pl.when(b != z)
        def _():
            pltpu.make_async_remote_copy(
                src_ref=blocks.at[b], dst_ref=blocks.at[b], send_sem=sz.at[0], recv_sem=rz.at[b],
                device_id=(kv, tp), device_id_type=MESH,
            ).wait_recv()

        q = blocks[b]
        total = jnp.zeros((96, 128), F32)
        out = jnp.zeros((96, HD), F32)
        for c in range(8):
            at = pl.ds(c * CHUNK, CHUNK)
            e = jnp.exp2(jnp.tanh(nt(q, kv_v[0, at]) * sc_v[0, :, at]) * (50.0 * LOG2E))
            total += e[:, :128] + e[:, 128:]
            out += mm((e * sc_v[1, :, at]).astype(BF), kv_v[1, at])
        high, low = split(total)
        wide = mm(expand, jnp.concatenate([out.astype(BF), high, low], axis=1))
        totals = nt(ones, wide[:, 128:].astype(BF))
        high, low = split(totals)
        msg = jnp.where(in_slab == 12, high.astype(F32), jnp.where(in_slab == 13, low.astype(F32), wide[:, :HD]))
        msgs[b] = msg.astype(BF).reshape(NPRE, SLAB, HD)
        for i in (4, 3, 5, 2, 6, 1, 7):
            back_to(b, i).start()

        @pl.when(b != z)
        def _():
            back_to(b, 0).start()

        @pl.when(b == z)
        def _():
            back[z, y] = msgs[z, y]

        return carry

    lax.fori_loop(0, nz, one_block, 0)

    def wait_back(j, carry):
        a, b = lax.div(j, ny), lax.rem(j, ny)

        @pl.when((a != z) | (b != y))
        def _():
            pltpu.make_async_remote_copy(
                src_ref=back.at[a, b], dst_ref=back.at[a, b], send_sem=sr.at[0, 0], recv_sem=rr.at[a, b],
                device_id=(kv, tp), device_id_type=MESH,
            ).wait_recv()

        return carry

    lax.fori_loop(0, nz * ny, wait_back, 0)
    summed = back[0].astype(F32)
    for a in range(1, 8):
        summed += back[a].astype(F32)
    high, low = split(summed.reshape(128, HD))
    held = jnp.concatenate([high, low], axis=0)
    lane = iota((16, 256), 1) & 127
    first = (ids * SLAB).astype(jnp.int32)
    picks = [jnp.where(lane == place + h * SLOTS, 1.0, 0.0) for h in range(2)]
    pick_total = jnp.where((lane == first + 12) | (lane == first + 13), 1.0, 0.0)
    found = mm(jnp.concatenate([picks[0], picks[1], pick_total, pick_total], axis=0).astype(BF), held)
    total_rows = found[32:]
    rank_lane = y * SLAB + rank.astype(jnp.int32)
    total = jnp.concatenate(
        [
            jnp.sum(jnp.where(lane16 == rank_lane + h * SLOTS, total_rows[:16], 0.0), axis=1, keepdims=True)
            for h in range(2)
        ],
        axis=0,
    )
    att = ((found[:32] + suf_out) / (total + suf_total)).astype(BF)
    att = jnp.concatenate([att[:16], att[16:]], axis=1)

    got_w.wait()

    def to_group(i, c):
        return pltpu.make_async_remote_copy(
            src_ref=part.at[i, c], dst_ref=parts.at[tp], send_sem=sx.at[i, c], recv_sem=rx.at[tp],
            device_id=(kv, lax.rem(x + i, nx) * 2 + c), device_id_type=MESH,
        )

    for i in (2, 1, 3, 0):
        at = pl.multiple_of(lax.rem(x + i, nx) * 1152, 128)
        got = mm(att, w_v[:, pl.ds(at, 1152)])
        part[i, 0] = got[:, :640].astype(BF)
        part[i, 1] = got[:, 512:].astype(BF)
        if i:
            to_group(i, 0).start()
            to_group(i, 1).start()
        else:
            own = jnp.where(core == 0, got[:, :640], got[:, 512:])
            pltpu.make_async_remote_copy(
                src_ref=part.at[0, 1 - core], dst_ref=parts.at[tp], send_sem=sx.at[0, 0], recv_sem=rx.at[tp],
                device_id=(kv, x * 2 + (1 - core)), device_id_type=MESH,
            ).start()
    got_res.wait()
    got_gain.wait()
    for i in range(1, 8):
        t = lax.rem(tp + i, 8)
        pltpu.make_async_remote_copy(
            src_ref=parts.at[t], dst_ref=parts.at[t], send_sem=sx.at[0, 0], recv_sem=rx.at[t],
            device_id=(kv, tp), device_id_type=MESH,
        ).wait_recv()
        own += parts[t].astype(F32)
    own = jnp.where(core == 0, own[:, :576], own[:, 64:])
    square[...] = jnp.broadcast_to(jnp.sum(own * own, axis=1, keepdims=True), (16, 128))

    def to_square(i):
        return pltpu.make_async_remote_copy(
            src_ref=square, dst_ref=squares.at[tp], send_sem=ss.at[i], recv_sem=rs.at[tp],
            device_id=(kv, lax.rem(tp + i, 8)), device_id_type=MESH,
        )

    for i in (4, 5, 3, 2, 6, 1, 7):
        to_square(i).start()
    resid = res_v[...].astype(F32)
    gained = own * gain_v[...].reshape(1, 576)
    sq = square[...]
    for i in range(1, 8):
        t = lax.rem(tp + i, 8)
        pltpu.make_async_remote_copy(
            src_ref=square, dst_ref=squares.at[t], send_sem=ss.at[0], recv_sem=rs.at[t],
            device_id=(kv, tp), device_id_type=MESH,
        ).wait_recv()
        sq += squares[t]
    scale = lax.rsqrt(sq[:, :1] / 4608.0 + 1e-06)
    o_ref[...] = (resid + gained * scale).astype(BF)

    for i in range(1, 8):
        to_holder(i).wait_send()
        along_row(i).wait_send()
        to_square(i).wait_send()
    for i in range(1, nx):
        to_group(i, 0).wait_send()
        to_group(i, 1).wait_send()
    to_group(0, 0).wait_send()

    def wait_sent(j, carry):
        b, i = lax.div(j, ny), lax.rem(j, ny)

        @pl.when((b != z) | (i != 0))
        def _():
            back_to(b, i).wait_send()

        return carry

    lax.fori_loop(0, nz * ny, wait_sent, 0)


def local(q, ids, kv, scales, suf, lens, w, res, gain):
    nz = ny = 8
    nx = lax.axis_size("tp") // 2
    hbm = pl.BlockSpec(memory_space=pl.ANY)
    vmem = pl.BlockSpec(memory_space=pltpu.VMEM)
    dma = pltpu.SemaphoreType.DMA

    def body(*refs):
        kernel(nz, ny, nx, *refs)

    return pl.pallas_call(
        body,
        out_shape=jax.ShapeDtypeStruct(res.shape, BF),
        in_specs=[hbm, vmem, hbm, hbm, hbm, vmem, hbm, hbm, hbm],
        out_specs=vmem,
        scratch_shapes=[
            pltpu.VMEM((16, 256), BF),
            pltpu.VMEM((2, 2048, 128), BF),
            pltpu.VMEM((2, 1, 2048), F32),
            pltpu.VMEM((2, 16, 128, 128), BF),
            pltpu.VMEM((256, 4608), BF),
            pltpu.VMEM((16, 576), BF),
            pltpu.VMEM((576,), F32),
            pltpu.VMEM((8, 16, 128), BF),
            pltpu.VMEM((8, 16, 128), BF),
            pltpu.VMEM((8, 96, 128), BF),
            pltpu.VMEM((8, 8, 16, 128), BF),
            pltpu.VMEM((8, 8, 16, 128), BF),
            pltpu.VMEM((4, 2, 16, 640), BF),
            pltpu.VMEM((8, 16, 640), BF),
            pltpu.VMEM((16, 128), F32),
            pltpu.VMEM((8, 16, 128), F32),
            pltpu.VMEM((16, 576), BF),
            dma((7,)),
            pltpu.SemaphoreType.REGULAR,
            pltpu.SemaphoreType.REGULAR,
            dma((8,)), dma((8,)), dma((8,)), dma((8,)),
            dma((8, 8)), dma((8, 8)),
            dma((4, 2)), dma((8,)), dma((8,)), dma((8,)),
        ],
        compiler_params=pltpu.CompilerParams(
            collective_id=0, has_side_effects=True, vmem_limit_bytes=62 * 2**20
        ),
        cost_estimate=pl.CostEstimate(flops=10**9, bytes_accessed=5 * 10**6, transcendentals=3 * 10**6),
        name="attend",
    )(q, ids.reshape(1, 16), kv, scales, suf, lens.reshape(1, 16), w, res, gain)


def solution(mesh):
    placed = (
        P("kv", "tp"), P("kv", None), P(None, "kv", "tp"), P(None, "tp", "kv"), P(None, "kv", None, "tp"),
        P("kv"), P("tp", None), P("kv", "tp"), P("tp"),
    )
    return jax.shard_map(local, mesh=mesh, in_specs=placed, out_specs=P("kv", "tp"), check_vma=False)
```

time: 533 us -> 46.6 us (0.09); the launches traced: 526 us -> 46.1 us
  blocking collectives: 335 us -> 0 us
  waiting for transfers between devices: 142 us -> 0 us
  Pallas kernels: 0 us -> 44.8 us
  matrix products: 18.2 us -> 0 us
  between operations: 14.9 us -> 0.01 us
  local copies, waits for them, and re-layouts: 13 us -> 1.34 us
    unnamed x2 -> x0, blocking collectives: 272 us -> none
    reduce_scatter x1 -> x0, waiting for transfers between devices: 103 us -> none  [local(): lax.psum_scatter(all_out, 'kv', scatter_dimension=0, tiled=True)]
    all_gather x1 -> x0, blocking collectives: 49.7 us -> none  [local(): lax.all_gather(queries, 'kv', axis=0, tiled=True)]
    pallas_call x0 -> x1, Pallas kernels: none -> 44.8 us  [local(): pl.pallas_call(body, out_shape=jax.ShapeDtypeStruct(res.shape, BF), in_sp...]
    unnamed x3 -> x0, waiting for transfers between devices: 38.9 us -> none
    dot_general x10 -> x0, matrix products: 15 us -> none  [the longest x4 10.4 us: prefix_terms(): lax.dot_general(head_rows, prefix_kv[0, :, columns], (((1,), (1,)), ((),...]
    psum x1 -> x0, blocking collectives: 12.9 us -> none  [local(): lax.psum(jnp.sum(own_projection * own_projection, axis=1), 'tp')]
    dynamic_update_slice x8 -> x0, local copies, waits for them, and re-layouts: 5.55 us -> none  [local(): lax.map(block_terms, gathered.reshape(block_count, block_rows, feature_co...]
  transfers between devices with their start and end apart: 2 -> 0, of which waited for: 2 -> 0; matrix products, arithmetic and copies ran while one was open for 1% -> 0% of each run, Pallas kernels for 0% -> 0%
where the time goes in v1:
time: 46.6 us; the launch traced here: 46.1 us
  Pallas kernels  44.8 us (96%)
  local copies, waits for them, and re-layouts  1.34 us (3%)
    pallas_call x1, Pallas kernels, local(): pl.pallas_call(body, out_shape=jax.ShapeDtypeStruct(res.shape, BF), in_sp...  44.8 us
    unnamed x1, local copies, waits for them, and re-layouts  1.34 us

profile of v1, /device:TPU:448, one launch (start us, length us, event | category | flops | bytes accessed | tf_op | source)
XLA Modules:
  0.0 46.1 jit_solution(8678890911575809729)
XLA Ops:
  0.0 44.8 %attend.1 = bf16[16,576]{1,0:T(8,128)(2,1)} custom-call(bf16[16,256]{1,0:T(8,128)(2,1)} %refs_0_.1, s32[1,16]{1,0:T(1,128)} %bitcast.2, bf16[2,2048,128]{2,1,0:T(8,128)(2,1)} %refs_2_.1, f32[2,1,2048]{2,1,0:T(1,128)} %refs_3_.1, bf16[2,16,128,128]{3,2,1,0:T(8,128)(2,1)} %refs_4_.1, s32[1,16]{1,0:T(1,128)} %bitcast.3, bf16[256,4608]{1,0:T(8,128)(2,1)} %refs_6_.1, ...), custom_call_target="tpu_custom_call" | custom-call | flops 1000000000 | bytes 5000000 | tf_op jit(solution)/shard_map/attend/pallas_call | solution.py:337
  44.8 1.3 %copy.11 = bf16[16,576]{1,0:T(8,128)(2,1)} copy(bf16[16,576]{1,0:T(8,128)(2,1)} %attend.1) | data formatting | bytes 36864

commit v2 on v1

--- a/solution.py
+++ b/solution.py
@@ -38,7 +38,7 @@
     nz, ny, nx,
     q_ref, ids_ref, kv_ref, scales_ref, suf_ref, len_ref, w_ref, res_ref, gain_ref,
     o_ref,
-    q_v, kv_v, sc_v, suf_v, w_v, res_v, gain_v,
+    q_v, ids_v, len_v, kv_v, sc_v, suf_v, w_v, res_v, gain_v,
     slots, gathered, blocks, msgs, back, part, parts, square, squares, out_v,
     local_sem, go_y, go_z, sy, ry, sz, rz, sr, rr, sx, rx, ss, rs,
 ):
@@ -53,9 +53,9 @@
 
     here(kv, x * 2 + (1 - core))
     for i in (4, 3, 5, 2, 6, 1, 7):
+        here(lax.rem(y + i, ny) * nz + z, x * 2)
+    for i in (4, 3, 5, 2, 6, 1, 7):
         here(y * nz + lax.rem(z + i, nz), x * 2 + 1)
-    for i in (4, 3, 5, 2, 6, 1, 7):
-        here(lax.rem(y + i, ny) * nz + z, x * 2)
     for i in (2, 1, 3):
         here(kv, lax.rem(x + i, nx) * 2 + 1)
 
@@ -65,6 +65,8 @@
         return c
 
     got_q = fetch(0, q_ref, q_v)
+    got_ids = fetch(7, ids_ref, ids_v)
+    got_len = fetch(8, len_ref, len_v)
     got_kv = fetch(1, kv_ref, kv_v)
     got_sc = fetch(2, scales_ref, sc_v)
     got_suf = fetch(3, suf_ref, suf_v)
@@ -73,7 +75,8 @@
     got_gain = fetch(6, gain_ref, gain_v)
 
     row16, lane16 = iota((16, 128), 0), iota((16, 128), 1)
-    ids_row = ids_ref[...].astype(F32)
+    got_ids.wait()
+    ids_row = ids_v[...].astype(F32)
     square16 = iota((16, 16), 0), iota((16, 16), 1)
     ids = jnp.sum(jnp.where(square16[0] == square16[1], ids_row, 0.0), axis=1, keepdims=True)
     same = jnp.where(ids == ids_row, 1.0, 0.0)
@@ -100,17 +103,18 @@
     def to_holder(i):
         p = lax.rem(y + i, ny)
         return pltpu.make_async_remote_copy(
-            src_ref=slots.at[p], dst_ref=gathered.at[y], send_sem=sy.at[i], recv_sem=ry.at[y],
+            src_ref=slots.at[p], dst_ref=gathered.at[y], send_sem=sy.at[i], recv_sem=ry,
             device_id=(p * nz + z, tp), device_id_type=MESH,
         )
 
     for i in (4, 3, 5, 2, 6, 1, 7):
         to_holder(i).start()
-    gathered[y] = slots[y]
+    pltpu.make_async_copy(slots.at[y], gathered.at[y], ry).start()
 
     got_suf.wait()
+    got_len.wait()
     eye = jnp.where(iota((32, 16), 1) == lax.rem(iota((32, 16), 0), 16), 1.0, 0.0)
-    lens = jnp.sum(eye * len_ref[...].astype(F32), axis=1, keepdims=True).astype(jnp.int32)
+    lens = jnp.sum(eye * len_v[...].astype(F32), axis=1, keepdims=True).astype(jnp.int32)
     own_q = jnp.concatenate([q_v[:, :HD], q_v[:, HD:]], axis=0)
     own_request = lax.rem(iota((32, CHUNK), 0), 16)
     suf_out = jnp.zeros((32, HD), F32)
@@ -130,14 +134,7 @@
     got_sc.wait()
     sc_v[0] = sc_v[0] * (SCORE / 50.0)
 
-    def from_source(i):
-        return pltpu.make_async_remote_copy(
-            src_ref=slots.at[i], dst_ref=gathered.at[i], send_sem=sy.at[i], recv_sem=ry.at[i],
-            device_id=(kv, tp), device_id_type=MESH,
-        )
-
-    for i in range(1, ny):
-        from_source(lax.rem(y + i, ny)).wait_recv()
+    pltpu.make_async_copy(gathered, gathered, ry).wait()
     compact = jnp.where(
         iota((96, 128), 1) == lax.div(iota((96, 128), 0), 12) * SLAB + lax.rem(iota((96, 128), 0), 12), 1.0, 0.0
     ).astype(BF)
@@ -172,60 +169,57 @@
     def back_to(b, i):
         to_y = lax.rem(y + i, ny)
         return pltpu.make_async_remote_copy(
-            src_ref=msgs.at[b, to_y], dst_ref=back.at[z, y], send_sem=sr.at[b, i], recv_sem=rr.at[z, y],
+            src_ref=msgs.at[b * ny + to_y], dst_ref=back.at[z, y], send_sem=sr, recv_sem=rr,
             device_id=(to_y * nz + b, tp), device_id_type=MESH,
         )
 
-    def one_block(b, carry):
-        @pl.when(b != z)
-        def _():
-            pltpu.make_async_remote_copy(
-                src_ref=blocks.at[b], dst_ref=blocks.at[b], send_sem=sz.at[0], recv_sem=rz.at[b],
-                device_id=(kv, tp), device_id_type=MESH,
-            ).wait_recv()
-
-        q = blocks[b]
-        total = jnp.zeros((96, 128), F32)
-        out = jnp.zeros((96, HD), F32)
-        for c in range(8):
-            at = pl.ds(c * CHUNK, CHUNK)
+    def two_blocks(step, carry):
+        for j in range(2):
+            b = step * 2 + j
+
+            @pl.when(b != z)
+            def _():
+                pltpu.make_async_remote_copy(
+                    src_ref=blocks.at[b], dst_ref=blocks.at[b], send_sem=sz.at[0], recv_sem=rz.at[b],
+                    device_id=(kv, tp), device_id_type=MESH,
+                ).wait_recv()
+
+        q = blocks[pl.ds(step * 2, 2)].reshape(192, HD)
+        total = jnp.zeros((192, 128), F32)
+        out = jnp.zeros((192, HD), F32)
+        for n in range(2):
+            at = pl.ds(n * 1024, 1024)
             e = jnp.exp2(jnp.tanh(nt(q, kv_v[0, at]) * sc_v[0, :, at]) * (50.0 * LOG2E))
-            total += e[:, :128] + e[:, 128:]
+            for c in range(8):
+                total += e[:, c * 128 : (c + 1) * 128]
             out += mm((e * sc_v[1, :, at]).astype(BF), kv_v[1, at])
         high, low = split(total)
-        wide = mm(expand, jnp.concatenate([out.astype(BF), high, low], axis=1))
-        totals = nt(ones, wide[:, 128:].astype(BF))
-        high, low = split(totals)
-        msg = jnp.where(in_slab == 12, high.astype(F32), jnp.where(in_slab == 13, low.astype(F32), wide[:, :HD]))
-        msgs[b] = msg.astype(BF).reshape(NPRE, SLAB, HD)
-        for i in (4, 3, 5, 2, 6, 1, 7):
-            back_to(b, i).start()
-
-        @pl.when(b != z)
-        def _():
-            back_to(b, 0).start()
-
-        @pl.when(b == z)
-        def _():
-            back[z, y] = msgs[z, y]
+        rows = jnp.concatenate([out.astype(BF), high, low], axis=1)
+        for j in range(2):
+            b = step * 2 + j
+            wide = mm(expand, rows[j * 96 : j * 96 + 96])
+            totals = nt(ones, wide[:, 128:].astype(BF))
+            high, low = split(totals)
+            msg = jnp.where(in_slab == 12, high.astype(F32), jnp.where(in_slab == 13, low.astype(F32), wide[:, :HD]))
+            msgs[pl.ds(b * ny, ny)] = msg.astype(BF).reshape(NPRE, SLAB, HD)
+        for j in range(2):
+            b = step * 2 + j
+            for i in (4, 3, 5, 2, 6, 1, 7):
+                back_to(b, i).start()
+
+            @pl.when(b != z)
+            def _():
+                back_to(b, 0).start()
+
+            @pl.when(b == z)
+            def _():
+                pltpu.make_async_copy(msgs.at[z * ny + y], back.at[z, y], rr).start()
 
         return carry
 
-    lax.fori_loop(0, nz, one_block, 0)
-
-    def wait_back(j, carry):
-        a, b = lax.div(j, ny), lax.rem(j, ny)
-
-        @pl.when((a != z) | (b != y))
-        def _():
-            pltpu.make_async_remote_copy(
-                src_ref=back.at[a, b], dst_ref=back.at[a, b], send_sem=sr.at[0, 0], recv_sem=rr.at[a, b],
-                device_id=(kv, tp), device_id_type=MESH,
-            ).wait_recv()
-
-        return carry
-
-    lax.fori_loop(0, nz * ny, wait_back, 0)
+    lax.fori_loop(0, nz // 2, two_blocks, 0)
+
+    pltpu.make_async_copy(back, back, rr).wait()
     summed = back[0].astype(F32)
     for a in range(1, 8):
         summed += back[a].astype(F32)
@@ -280,7 +274,9 @@
         ).wait_recv()
         own += parts[t].astype(F32)
     own = jnp.where(core == 0, own[:, :576], own[:, 64:])
-    square[...] = jnp.broadcast_to(jnp.sum(own * own, axis=1, keepdims=True), (16, 128))
+    square[...] = jnp.sum(
+        jnp.where(row16 == lane16, jnp.sum(own * own, axis=1, keepdims=True), 0.0), axis=0, keepdims=True
+    )
 
     def to_square(i):
         return pltpu.make_async_remote_copy(
@@ -300,7 +296,8 @@
             device_id=(kv, tp), device_id_type=MESH,
         ).wait_recv()
         sq += squares[t]
-    scale = lax.rsqrt(sq[:, :1] / 4608.0 + 1e-06)
+    sq = jnp.sum(jnp.where(row16 == lane16, sq, 0.0), axis=1, keepdims=True)
+    scale = lax.rsqrt(sq / 4608.0 + 1e-06)
     o_ref[...] = (resid + gained * scale).astype(BF)
 
     for i in range(1, 8):
@@ -312,16 +309,8 @@
         to_group(i, 1).wait_send()
     to_group(0, 0).wait_send()
 
-    def wait_sent(j, carry):
-        b, i = lax.div(j, ny), lax.rem(j, ny)
-
-        @pl.when((b != z) | (i != 0))
-        def _():
-            back_to(b, i).wait_send()
-
-        return carry
-
-    lax.fori_loop(0, nz * ny, wait_sent, 0)
+    sent = msgs.at[pl.ds(0, nz * ny - 1)]
+    pltpu.make_async_copy(sent, sent, sr).wait()
 
 
 def local(q, ids, kv, scales, suf, lens, w, res, gain):
@@ -337,10 +326,12 @@
     return pl.pallas_call(
         body,
         out_shape=jax.ShapeDtypeStruct(res.shape, BF),
-        in_specs=[hbm, vmem, hbm, hbm, hbm, vmem, hbm, hbm, hbm],
+        in_specs=[hbm] * 9,
         out_specs=vmem,
         scratch_shapes=[
             pltpu.VMEM((16, 256), BF),
+            pltpu.VMEM((1, 16), jnp.int32),
+            pltpu.VMEM((1, 16), jnp.int32),
             pltpu.VMEM((2, 2048, 128), BF),
             pltpu.VMEM((2, 1, 2048), F32),
             pltpu.VMEM((2, 16, 128, 128), BF),
@@ -350,18 +341,18 @@
             pltpu.VMEM((8, 16, 128), BF),
             pltpu.VMEM((8, 16, 128), BF),
             pltpu.VMEM((8, 96, 128), BF),
-            pltpu.VMEM((8, 8, 16, 128), BF),
+            pltpu.VMEM((64, 16, 128), BF),
             pltpu.VMEM((8, 8, 16, 128), BF),
             pltpu.VMEM((4, 2, 16, 640), BF),
             pltpu.VMEM((8, 16, 640), BF),
-            pltpu.VMEM((16, 128), F32),
-            pltpu.VMEM((8, 16, 128), F32),
+            pltpu.VMEM((1, 128), F32),
+            pltpu.VMEM((8, 1, 128), F32),
             pltpu.VMEM((16, 576), BF),
-            dma((7,)),
+            dma((9,)),
             pltpu.SemaphoreType.REGULAR,
             pltpu.SemaphoreType.REGULAR,
-            dma((8,)), dma((8,)), dma((8,)), dma((8,)),
-            dma((8, 8)), dma((8, 8)),
+            dma((8,)), dma, dma((8,)), dma((8,)),
+            dma, dma,
             dma((4, 2)), dma((8,)), dma((8,)), dma((8,)),
         ],
         compiler_params=pltpu.CompilerParams(

time: 46.6 us -> 43 us (0.923)
  Pallas kernels: 44.8 us -> 41.5 us
    pallas_call x1, Pallas kernels: 44.8 us -> 41.5 us  [local(): pl.pallas_call(body, out_shape=jax.ShapeDtypeStruct(res.shape, BF), in_sp...]
where the time goes in v2:
time: 43 us; the launch traced here: 42.9 us
  Pallas kernels  41.5 us (97%)
  local copies, waits for them, and re-layouts  1.34 us (3%)
    pallas_call x1, Pallas kernels, local(): pl.pallas_call(body, out_shape=jax.ShapeDtypeStruct(res.shape, BF), in_sp...  41.5 us
    unnamed x1, local copies, waits for them, and re-layouts  1.34 us

profile of v2, /device:TPU:448, one launch (start us, length us, event | category | flops | bytes accessed | tf_op | source)
XLA Modules:
  0.0 42.9 jit_solution(787433560264931429)
XLA Ops:
  0.0 41.5 %attend.1 = bf16[16,576]{1,0:T(8,128)(2,1)} custom-call(bf16[16,256]{1,0:T(8,128)(2,1)} %refs_0_.1, s32[1,16]{1,0:T(1,128)} %bitcast.2, bf16[2,2048,128]{2,1,0:T(8,128)(2,1)} %refs_2_.1, f32[2,1,2048]{2,1,0:T(1,128)} %refs_3_.1, bf16[2,16,128,128]{3,2,1,0:T(8,128)(2,1)} %refs_4_.1, s32[1,16]{1,0:T(1,128)} %bitcast.3, bf16[256,4608]{1,0:T(8,128)(2,1)} %refs_6_.1, ...), custom_call_target="tpu_custom_call" | custom-call | flops 1000000000 | bytes 5000000 | tf_op jit(solution)/shard_map/attend/pallas_call | solution.py:326
  41.5 1.3 %copy.11 = bf16[16,576]{1,0:T(8,128)(2,1)} copy(bf16[16,576]{1,0:T(8,128)(2,1)} %attend.1) | data formatting | bytes 36864

commit v3 on v2

--- a/solution.py
+++ b/solution.py
@@ -51,11 +51,12 @@
     def here(to_kv, to_tp):
         pl.semaphore_signal(barrier, inc=1, device_id=(to_kv, to_tp), device_id_type=MESH)
 
+    late = nz // 2
     here(kv, x * 2 + (1 - core))
     for i in (4, 3, 5, 2, 6, 1, 7):
         here(lax.rem(y + i, ny) * nz + z, x * 2)
     for i in (4, 3, 5, 2, 6, 1, 7):
-        here(y * nz + lax.rem(z + i, nz), x * 2 + 1)
+        here(y * nz + lax.rem(z + i, nz), x * 2 + jnp.where(z < late, 0, 1))
     for i in (2, 1, 3):
         here(kv, lax.rem(x + i, nx) * 2 + 1)
 
@@ -93,7 +94,7 @@
 
     @pl.when(core == 0)
     def _():
-        pl.semaphore_wait(barrier, 2 * (ny - 1) + 1)
+        pl.semaphore_wait(barrier, 1 + 2 * (ny - 1) + 2 * jnp.where(z < late, late - 1, late))
         pl.semaphore_signal(go_y, inc=1, device_id=(kv, tp + 1), device_id_type=MESH)
 
     @pl.when(core == 1)
@@ -140,23 +141,32 @@
     ).astype(BF)
     blocks[z] = mm(compact, gathered[...].reshape(128, HD)).astype(BF)
 
+    def along_row(i):
+        return pltpu.make_async_remote_copy(
+            src_ref=blocks.at[z], dst_ref=blocks.at[z], send_sem=sz.at[i], recv_sem=rz.at[z],
+            device_id=(y * nz + lax.rem(z + i, nz), tp), device_id_type=MESH,
+        )
+
+    def to_half(half):
+        for i in (4, 3, 5, 2, 6, 1, 7):
+
+            @pl.when(lax.div(lax.rem(z + i, nz), late) == half)
+            def _():
+                along_row(i).start()
+
+    to_half(0)
+
     @pl.when(core == 1)
     def _():
-        pl.semaphore_wait(barrier, 2 * (nz - 1) + 1 + 2 * (nx - 1))
+        pl.semaphore_wait(barrier, 1 + 2 * (nx - 1) + 2 * jnp.where(z < late, late, late - 1))
         pl.semaphore_signal(go_z, inc=1, device_id=(kv, tp - 1), device_id_type=MESH)
 
     @pl.when(core == 0)
     def _():
         pl.semaphore_wait(go_z, 1)
 
-    def along_row(i):
-        return pltpu.make_async_remote_copy(
-            src_ref=blocks.at[z], dst_ref=blocks.at[z], send_sem=sz.at[i], recv_sem=rz.at[z],
-            device_id=(y * nz + lax.rem(z + i, nz), tp), device_id_type=MESH,
-        )
-
-    for i in (4, 3, 5, 2, 6, 1, 7):
-        along_row(i).start()
+    to_half(1)
+
 
     expand = jnp.where(
         (iota((128, 96), 1) == lax.div(iota((128, 96), 0), SLAB) * 12 + lax.rem(iota((128, 96), 0), SLAB))
@@ -173,51 +183,41 @@
             device_id=(to_y * nz + b, tp), device_id_type=MESH,
         )
 
-    def two_blocks(step, carry):
-        for j in range(2):
-            b = step * 2 + j
-
-            @pl.when(b != z)
-            def _():
-                pltpu.make_async_remote_copy(
-                    src_ref=blocks.at[b], dst_ref=blocks.at[b], send_sem=sz.at[0], recv_sem=rz.at[b],
-                    device_id=(kv, tp), device_id_type=MESH,
-                ).wait_recv()
-
-        q = blocks[pl.ds(step * 2, 2)].reshape(192, HD)
-        total = jnp.zeros((192, 128), F32)
-        out = jnp.zeros((192, HD), F32)
-        for n in range(2):
-            at = pl.ds(n * 1024, 1024)
-            e = jnp.exp2(jnp.tanh(nt(q, kv_v[0, at]) * sc_v[0, :, at]) * (50.0 * LOG2E))
-            for c in range(8):
-                total += e[:, c * 128 : (c + 1) * 128]
-            out += mm((e * sc_v[1, :, at]).astype(BF), kv_v[1, at])
+    def one_block(b, carry):
+        @pl.when(b != z)
+        def _():
+            pltpu.make_async_remote_copy(
+                src_ref=blocks.at[b], dst_ref=blocks.at[b], send_sem=sz.at[0], recv_sem=rz.at[b],
+                device_id=(kv, tp), device_id_type=MESH,
+            ).wait_recv()
+
+        q = blocks[b]
+        total = jnp.zeros((96, 128), F32)
+        out = jnp.zeros((96, HD), F32)
+        e = jnp.exp2(jnp.tanh(nt(q, kv_v[0]) * sc_v[0]) * (50.0 * LOG2E))
+        for c in range(16):
+            total += e[:, c * 128 : (c + 1) * 128]
+        out += mm((e * sc_v[1]).astype(BF), kv_v[1])
         high, low = split(total)
-        rows = jnp.concatenate([out.astype(BF), high, low], axis=1)
-        for j in range(2):
-            b = step * 2 + j
-            wide = mm(expand, rows[j * 96 : j * 96 + 96])
-            totals = nt(ones, wide[:, 128:].astype(BF))
-            high, low = split(totals)
-            msg = jnp.where(in_slab == 12, high.astype(F32), jnp.where(in_slab == 13, low.astype(F32), wide[:, :HD]))
-            msgs[pl.ds(b * ny, ny)] = msg.astype(BF).reshape(NPRE, SLAB, HD)
-        for j in range(2):
-            b = step * 2 + j
-            for i in (4, 3, 5, 2, 6, 1, 7):
-                back_to(b, i).start()
-
-            @pl.when(b != z)
-            def _():
-                back_to(b, 0).start()
-
-            @pl.when(b == z)
-            def _():
-                pltpu.make_async_copy(msgs.at[z * ny + y], back.at[z, y], rr).start()
+        wide = mm(expand, jnp.concatenate([out.astype(BF), high, low], axis=1))
+        totals = nt(ones, wide[:, 128:].astype(BF))
+        high, low = split(totals)
+        msg = jnp.where(in_slab == 12, high.astype(F32), jnp.where(in_slab == 13, low.astype(F32), wide[:, :HD]))
+        msgs[pl.ds(b * ny, ny)] = msg.astype(BF).reshape(NPRE, SLAB, HD)
+        for i in (4, 3, 5, 2, 6, 1, 7):
+            back_to(b, i).start()
+
+        @pl.when(b != z)
+        def _():
+            back_to(b, 0).start()
+
+        @pl.when(b == z)
+        def _():
+            pltpu.make_async_copy(msgs.at[z * ny + y], back.at[z, y], rr).start()
 
         return carry
 
-    lax.fori_loop(0, nz // 2, two_blocks, 0)
+    lax.fori_loop(0, nz, one_block, 0)
 
     pltpu.make_async_copy(back, back, rr).wait()
     summed = back[0].astype(F32)

time: 43 us -> 42 us (0.977)
  Pallas kernels: 41.5 us -> 40.2 us
    pallas_call x1, Pallas kernels: 41.5 us -> 40.2 us  [local(): pl.pallas_call(body, out_shape=jax.ShapeDtypeStruct(res.shape, BF), in_sp...]
where the time goes in v3:
time: 42 us; the launch traced here: 41.6 us
  Pallas kernels  40.2 us (96%)
  local copies, waits for them, and re-layouts  1.34 us (3%)
    pallas_call x1, Pallas kernels, local(): pl.pallas_call(body, out_shape=jax.ShapeDtypeStruct(res.shape, BF), in_sp...  40.2 us
    unnamed x1, local copies, waits for them, and re-layouts  1.34 us

profile of v3, /device:TPU:448, one launch (start us, length us, event | category | flops | bytes accessed | tf_op | source)
XLA Modules:
  0.0 41.6 jit_solution(13942071957398394755)
XLA Ops:
  0.0 40.2 %attend.1 = bf16[16,576]{1,0:T(8,128)(2,1)} custom-call(bf16[16,256]{1,0:T(8,128)(2,1)} %refs_0_.1, s32[1,16]{1,0:T(1,128)} %bitcast.2, bf16[2,2048,128]{2,1,0:T(8,128)(2,1)} %refs_2_.1, f32[2,1,2048]{2,1,0:T(1,128)} %refs_3_.1, bf16[2,16,128,128]{3,2,1,0:T(8,128)(2,1)} %refs_4_.1, s32[1,16]{1,0:T(1,128)} %bitcast.3, bf16[256,4608]{1,0:T(8,128)(2,1)} %refs_6_.1, ...), custom_call_target="tpu_custom_call" | custom-call | flops 1000000000 | bytes 5000000 | tf_op jit(solution)/shard_map/attend/pallas_call | solution.py:326
  40.2 1.3 %copy.11 = bf16[16,576]{1,0:T(8,128)(2,1)} copy(bf16[16,576]{1,0:T(8,128)(2,1)} %attend.1) | data formatting | bytes 36864

commit v4 on v3

--- a/solution.py
+++ b/solution.py
@@ -156,24 +156,17 @@
 
     to_half(0)
 
-    @pl.when(core == 1)
-    def _():
-        pl.semaphore_wait(barrier, 1 + 2 * (nx - 1) + 2 * jnp.where(z < late, late, late - 1))
-        pl.semaphore_signal(go_z, inc=1, device_id=(kv, tp - 1), device_id_type=MESH)
-
-    @pl.when(core == 0)
-    def _():
-        pl.semaphore_wait(go_z, 1)
-
-    to_half(1)
-
-
     expand = jnp.where(
         (iota((128, 96), 1) == lax.div(iota((128, 96), 0), SLAB) * 12 + lax.rem(iota((128, 96), 0), SLAB))
         & (lax.rem(iota((128, 96), 0), SLAB) < 12),
         1.0, 0.0,
     ).astype(BF)
-    ones = jnp.ones((128, 256), BF)
+    ones = jnp.ones((16, 128), BF)
+    zeros = jnp.zeros((16, 32), F32)
+
+    def row_of_totals(a):
+        return jnp.concatenate([nt(ones, a), zeros], axis=1)
+
     in_slab = lax.rem(iota((128, 128), 0), SLAB)
 
     def back_to(b, i):
@@ -183,7 +176,22 @@
             device_id=(to_y * nz + b, tp), device_id_type=MESH,
         )
 
-    def one_block(b, carry):
+    def one_block(step, carry):
+        @pl.when(step == jnp.where(z < late, jnp.where(z == 2, 2, 1), 0))
+        def _():
+            @pl.when(core == 1)
+            def _():
+                pl.semaphore_wait(barrier, 1 + 2 * (nx - 1) + 2 * jnp.where(z < late, late, late - 1))
+                pl.semaphore_signal(go_z, inc=1, device_id=(kv, tp - 1), device_id_type=MESH)
+
+            @pl.when(core == 0)
+            def _():
+                pl.semaphore_wait(go_z, 1)
+
+            to_half(1)
+
+        b = jnp.where((z >= late) | (step > z), step, jnp.where(step == 0, z, step - 1))
+
         @pl.when(b != z)
         def _():
             pltpu.make_async_remote_copy(
@@ -199,10 +207,9 @@
             total += e[:, c * 128 : (c + 1) * 128]
         out += mm((e * sc_v[1]).astype(BF), kv_v[1])
         high, low = split(total)
-        wide = mm(expand, jnp.concatenate([out.astype(BF), high, low], axis=1))
-        totals = nt(ones, wide[:, 128:].astype(BF))
-        high, low = split(totals)
-        msg = jnp.where(in_slab == 12, high.astype(F32), jnp.where(in_slab == 13, low.astype(F32), wide[:, :HD]))
+        high, low = split(row_of_totals(high) + row_of_totals(low))
+        msg = mm(expand, out.astype(BF))
+        msg = jnp.where(in_slab == 12, high[:1].astype(F32), jnp.where(in_slab == 13, low[:1].astype(F32), msg))
         msgs[pl.ds(b * ny, ny)] = msg.astype(BF).reshape(NPRE, SLAB, HD)
         for i in (4, 3, 5, 2, 6, 1, 7):
             back_to(b, i).start()
@@ -219,22 +226,23 @@
 
     lax.fori_loop(0, nz, one_block, 0)
 
+    lane = iota((16, 256), 1) & 127
+    first = (ids * SLAB).astype(jnp.int32)
+    picks = [jnp.where(lane == place + h * SLOTS, 1.0, 0.0) for h in range(2)]
+    pick_total = jnp.where((lane == first + 12) | (lane == first + 13), 1.0, 0.0)
+    picks = jnp.concatenate([picks[0], picks[1], pick_total], axis=0).astype(BF)
     pltpu.make_async_copy(back, back, rr).wait()
     summed = back[0].astype(F32)
     for a in range(1, 8):
         summed += back[a].astype(F32)
     high, low = split(summed.reshape(128, HD))
     held = jnp.concatenate([high, low], axis=0)
-    lane = iota((16, 256), 1) & 127
-    first = (ids * SLAB).astype(jnp.int32)
-    picks = [jnp.where(lane == place + h * SLOTS, 1.0, 0.0) for h in range(2)]
-    pick_total = jnp.where((lane == first + 12) | (lane == first + 13), 1.0, 0.0)
-    found = mm(jnp.concatenate([picks[0], picks[1], pick_total, pick_total], axis=0).astype(BF), held)
+    found = mm(picks, held)
     total_rows = found[32:]
-    rank_lane = y * SLAB + rank.astype(jnp.int32)
+    rank_lane = y * 12 + rank.astype(jnp.int32)
     total = jnp.concatenate(
         [
-            jnp.sum(jnp.where(lane16 == rank_lane + h * SLOTS, total_rows[:16], 0.0), axis=1, keepdims=True)
+            jnp.sum(jnp.where(lane16 == rank_lane + h * SLOTS, total_rows, 0.0), axis=1, keepdims=True)
             for h in range(2)
         ],
         axis=0,
@@ -288,6 +296,18 @@
         to_square(i).start()
     resid = res_v[...].astype(F32)
     gained = own * gain_v[...].reshape(1, 576)
+    for i in range(1, 8):
+        to_holder(i).wait_send()
+        along_row(i).wait_send()
+        to_square(i).wait_send()
+    for i in range(1, nx):
+        to_group(i, 0).wait_send()
+        to_group(i, 1).wait_send()
+    to_group(0, 0).wait_send()
+
+    sent = msgs.at[pl.ds(0, nz * ny - 1)]
+    pltpu.make_async_copy(sent, sent, sr).wait()
+
     sq = square[...]
     for i in range(1, 8):
         t = lax.rem(tp + i, 8)
@@ -300,18 +320,6 @@
     scale = lax.rsqrt(sq / 4608.0 + 1e-06)
     o_ref[...] = (resid + gained * scale).astype(BF)
 
-    for i in range(1, 8):
-        to_holder(i).wait_send()
-        along_row(i).wait_send()
-        to_square(i).wait_send()
-    for i in range(1, nx):
-        to_group(i, 0).wait_send()
-        to_group(i, 1).wait_send()
-    to_group(0, 0).wait_send()
-
-    sent = msgs.at[pl.ds(0, nz * ny - 1)]
-    pltpu.make_async_copy(sent, sent, sr).wait()
-
 
 def local(q, ids, kv, scales, suf, lens, w, res, gain):
     nz = ny = 8
@@ -325,7 +333,7 @@
 
     return pl.pallas_call(
         body,
-        out_shape=jax.ShapeDtypeStruct(res.shape, BF),
+        out_shape=pltpu.VMEM(res.shape, BF),
         in_specs=[hbm] * 9,
         out_specs=vmem,
         scratch_shapes=[

time: 42 us -> 39.9 us (0.950)
  Pallas kernels: 40.2 us -> 39.2 us
  local copies, waits for them, and re-layouts: 1.34 us -> 0.61 us
    pallas_call x1, Pallas kernels: 40.2 us -> 39.2 us  [local(): pl.pallas_call(body, out_shape=pltpu.VMEM(res.shape, BF), in_specs=[hbm]...]
    unnamed x1, local copies, waits for them, and re-layouts: 1.34 us -> 0.61 us
where the time goes in v4:
time: 39.9 us; the launch traced here: 39.8 us
  Pallas kernels  39.2 us (98%)
  local copies, waits for them, and re-layouts  0.61 us (2%)
    pallas_call x1, Pallas kernels, local(): pl.pallas_call(body, out_shape=pltpu.VMEM(res.shape, BF), in_specs=[hbm]...  39.2 us

profile of v4, /device:TPU:448, one launch (start us, length us, event | category | flops | bytes accessed | tf_op | source)
XLA Modules:
  0.0 39.8 jit_solution(2507232678117520919)
XLA Ops:
  0.0 39.2 %attend.1 = bf16[16,576]{1,0:T(8,128)(2,1)S(1)} custom-call(bf16[16,256]{1,0:T(8,128)(2,1)} %refs_0_.1, s32[1,16]{1,0:T(1,128)} %bitcast.2, bf16[2,2048,128]{2,1,0:T(8,128)(2,1)} %refs_2_.1, f32[2,1,2048]{2,1,0:T(1,128)} %refs_3_.1, bf16[2,16,128,128]{3,2,1,0:T(8,128)(2,1)} %refs_4_.1, s32[1,16]{1,0:T(1,128)} %bitcast.3, bf16[256,4608]{1,0:T(8,128)(2,1)} %refs_6_.1, ...), custom_call_target="tpu_custom_call" | custom-call | flops 1000000000 | bytes 5000000 | tf_op jit(solution)/shard_map/attend/pallas_call | solution.py:334
  39.2 0.6 %copy.11 = bf16[16,576]{1,0:T(8,128)(2,1)} copy(bf16[16,576]{1,0:T(8,128)(2,1)S(1)} %attend.1) | data formatting | bytes 36864

commit v5 on v4

--- a/solution.py
+++ b/solution.py
@@ -190,7 +190,7 @@
 
             to_half(1)
 
-        b = jnp.where((z >= late) | (step > z), step, jnp.where(step == 0, z, step - 1))
+        b = jnp.where(z < late, jnp.where(step > z, step, jnp.where(step == 0, z, step - 1)), jnp.where(step == 1, 2, jnp.where(step == 2, 1, step)))
 
         @pl.when(b != z)
         def _():

time: 39.9 us -> 39.6 us (level)
  Pallas kernels: 39.2 us -> 38.7 us
    pallas_call x1, Pallas kernels: 39.2 us -> 38.7 us  [local(): pl.pallas_call(body, out_shape=pltpu.VMEM(res.shape, BF), in_specs=[hbm]...]
where the time goes in v5:
time: 39.6 us; the launch traced here: 39.3 us
  Pallas kernels  38.7 us (98%)
  local copies, waits for them, and re-layouts  0.61 us (2%)
    pallas_call x1, Pallas kernels, local(): pl.pallas_call(body, out_shape=pltpu.VMEM(res.shape, BF), in_specs=[hbm]...  38.7 us

profile of v5, /device:TPU:448, one launch (start us, length us, event | category | flops | bytes accessed | tf_op | source)
XLA Modules:
  0.0 39.3 jit_solution(14077219523481206020)
XLA Ops:
  0.0 38.7 %attend.1 = bf16[16,576]{1,0:T(8,128)(2,1)S(1)} custom-call(bf16[16,256]{1,0:T(8,128)(2,1)} %refs_0_.1, s32[1,16]{1,0:T(1,128)} %bitcast.2, bf16[2,2048,128]{2,1,0:T(8,128)(2,1)} %refs_2_.1, f32[2,1,2048]{2,1,0:T(1,128)} %refs_3_.1, bf16[2,16,128,128]{3,2,1,0:T(8,128)(2,1)} %refs_4_.1, s32[1,16]{1,0:T(1,128)} %bitcast.3, bf16[256,4608]{1,0:T(8,128)(2,1)} %refs_6_.1, ...), custom_call_target="tpu_custom_call" | custom-call | flops 1000000000 | bytes 5000000 | tf_op jit(solution)/shard_map/attend/pallas_call | solution.py:334
  38.7 0.6 %copy.11 = bf16[16,576]{1,0:T(8,128)(2,1)} copy(bf16[16,576]{1,0:T(8,128)(2,1)S(1)} %attend.1) | data formatting | bytes 36864

commit v6 on v5

--- a/solution.py
+++ b/solution.py
@@ -226,18 +226,13 @@
 
     lax.fori_loop(0, nz, one_block, 0)
 
-    lane = iota((16, 256), 1) & 127
+    lane = iota((16, 8 * 128), 1) & 127
     first = (ids * SLAB).astype(jnp.int32)
     picks = [jnp.where(lane == place + h * SLOTS, 1.0, 0.0) for h in range(2)]
     pick_total = jnp.where((lane == first + 12) | (lane == first + 13), 1.0, 0.0)
     picks = jnp.concatenate([picks[0], picks[1], pick_total], axis=0).astype(BF)
     pltpu.make_async_copy(back, back, rr).wait()
-    summed = back[0].astype(F32)
-    for a in range(1, 8):
-        summed += back[a].astype(F32)
-    high, low = split(summed.reshape(128, HD))
-    held = jnp.concatenate([high, low], axis=0)
-    found = mm(picks, held)
+    found = mm(picks, back[...].reshape(8 * 128, HD))
     total_rows = found[32:]
     rank_lane = y * 12 + rank.astype(jnp.int32)
     total = jnp.concatenate(

time: 39.6 us -> 39.6 us (level)
  no operation moved by 1% of the time
where the time goes in v6:
time: 39.6 us; the launch traced here: 39.3 us
  Pallas kernels  38.7 us (98%)
  local copies, waits for them, and re-layouts  0.61 us (2%)
    pallas_call x1, Pallas kernels, local(): pl.pallas_call(body, out_shape=pltpu.VMEM(res.shape, BF), in_specs=[hbm]...  38.7 us

profile of v6, /device:TPU:448, one launch (start us, length us, event | category | flops | bytes accessed | tf_op | source)
XLA Modules:
  0.0 39.3 jit_solution(12442255426708351279)
XLA Ops:
  0.0 38.7 %attend.1 = bf16[16,576]{1,0:T(8,128)(2,1)S(1)} custom-call(bf16[16,256]{1,0:T(8,128)(2,1)} %refs_0_.1, s32[1,16]{1,0:T(1,128)} %bitcast.2, bf16[2,2048,128]{2,1,0:T(8,128)(2,1)} %refs_2_.1, f32[2,1,2048]{2,1,0:T(1,128)} %refs_3_.1, bf16[2,16,128,128]{3,2,1,0:T(8,128)(2,1)} %refs_4_.1, s32[1,16]{1,0:T(1,128)} %bitcast.3, bf16[256,4608]{1,0:T(8,128)(2,1)} %refs_6_.1, ...), custom_call_target="tpu_custom_call" | custom-call | flops 1000000000 | bytes 5000000 | tf_op jit(solution)/shard_map/attend/pallas_call | solution.py:329
  38.7 0.6 %copy.11 = bf16[16,576]{1,0:T(8,128)(2,1)} copy(bf16[16,576]{1,0:T(8,128)(2,1)S(1)} %attend.1) | data formatting | bytes 36864
